TPU v7x, 512 devices: a whole 4x8x8 slice. The times are simulated.
512 devices in a mesh: pipe: 4 (over x), tm: 32 (over y_lo, z), dp: 4 (over y_hi, core).
Axes of the slice: x: 4, y: 8 (y_hi: 2, y_lo: 4; y = y_hi * 4 + y_lo), z: 8, core: 2. Of those that a mesh axis runs over, the one named last changes fastest.
Arguments:
- video: bfloat16 [4, 4, 64, 64, 320], P(None, 'dp', 'tm'), may hold values from -6 to 6
- cotangent: bfloat16 [4, 4, 64, 64, 320], P(None, 'dp', 'tm'), may hold values from -6 to 6
- timesteps: int32 [4, 4], P(None, 'dp'), may hold values from 0 to 999
- conv_weight: bfloat16 [4, 3, 320, 320], P('pipe'), may hold values from -0.1875 to 0.1875
- out_weight: bfloat16 [4, 320, 320], P('pipe'), may hold values from -0.3125 to 0.3125
Outputs:
- conv_grad: float32 [4, 3, 320, 320], P('pipe')
- out_grad: float32 [4, 320, 320], P('pipe')
All inputs are finite; a program needn't handle non-finite values.
Results may differ from a plain program's by a relative error of at most 0.012.
Values may be sent and summed in bfloat16 or wider, within the bound.
A program may use at most 64 MiB of HBM per device.

v0:
```python
import math
import jax
import jax.numpy as jnp
from jax import lax
from jax.sharding import PartitionSpec as P

EPSILON = 1e-06


def padded_2(block, sides, width):
    for axis, dim in sides:
        count = lax.axis_size(axis)
        forward = [(i, i + 1) for i in range(count - 1)]
        backward = [(target, source) for source, target in forward]
        low = lax.ppermute(
            lax.slice_in_dim(block, block.shape[dim] - width, None, axis=dim), axis, forward
        )
        high = lax.ppermute(lax.slice_in_dim(block, 0, width, axis=dim), axis, backward)
        block = jnp.concatenate([low, block, high], axis=dim)
    return block


def from_partner(value, axis, stride):
    mask = 2**stride
    pairs = [(source, source ^ mask) for source in range(lax.axis_size(axis))]
    return lax.ppermute(value, axis, pairs)


def from_behind(array, axis, by):
    peers = lax.axis_size(axis)
    pairs = [(i, i + by) for i in range(peers) if 0 <= i + by < peers]
    return lax.ppermute(array, axis, pairs)


def embed(times, channels):
    half = channels // 2
    index = jnp.arange(half).astype(jnp.float32)
    freq = jnp.exp(index * (-math.log(10000.0) / half))
    angle = times.astype(jnp.float32)[..., None] * freq
    return jnp.concatenate([jnp.sin(angle), jnp.cos(angle)], -1)


def prepare(inputs, emb_pair, conv_pair):
    x_float = inputs.astype(jnp.float32)
    inv_rms = lax.rsqrt(jnp.mean(x_float * x_float, -1, keepdims=True) + EPSILON)
    normed = x_float * inv_rms
    norm_low = normed.astype(jnp.bfloat16)
    padded = padded_2(norm_low, (("tm", 1),), 1)
    frames = inputs.shape[1]
    pre_act = emb_pair[:, None, None, :]
    for offset in range(3):
        pre_act = pre_act + jnp.einsum(
            "dfpc,dcx->dfpx",
            padded[:, offset : offset + frames],
            conv_pair[:, offset],
            preferred_element_type=jnp.float32,
        )
    active = jax.nn.silu(pre_act).astype(jnp.bfloat16)
    return (inv_rms, normed, padded, pre_act, active)


def body(video, cotangent, timesteps, conv_weight, out_weight):
    current_section_index = lax.axis_index("pipe")
    sections = lax.axis_size("pipe")
    final_section = sections - 1
    micro = video.shape[0]
    half_microbatch_count = micro // 2
    ticks = half_microbatch_count + sections - 1
    channels = video.shape[-1]
    frames = video.shape[2]
    bit_count = sections.bit_length() - 1
    packed = jnp.concatenate([conv_weight[0], out_weight[0][None]], 0)
    mirrored = packed
    for bit_pos in range(bit_count):
        mirrored = from_partner(mirrored, "pipe", bit_pos)
    conv_pair = jnp.stack([conv_weight[0], mirrored[:3]])
    out_pair = jnp.stack([out_weight[0], mirrored[3]])
    embedded = embed(timesteps[:, 0], channels)

    def pick(stacked, down_tick, up_tick):
        down_part = lax.dynamic_index_in_dim(
            stacked, jnp.clip(down_tick, 0, ticks - 1), 0, keepdims=False
        )[0]
        up_part = lax.dynamic_index_in_dim(
            stacked, jnp.clip(up_tick, 0, ticks - 1), 0, keepdims=False
        )[1]
        return jnp.stack([down_part, up_part])

    empty_activation = jnp.zeros(video.shape[2:], jnp.bfloat16)
    down_buf = empty_activation
    up_buf = empty_activation
    saved = []
    for current_clock_tick in range(ticks):
        down_in = down_buf
        up_in = up_buf
        if current_clock_tick < half_microbatch_count:
            down_in = jnp.where(current_section_index == 0, video[current_clock_tick, 0], down_buf)
            up_in = jnp.where(
                current_section_index == final_section,
                video[half_microbatch_count + current_clock_tick, 0],
                up_buf,
            )
        inputs = jnp.stack([down_in, up_in])
        down_row = lax.dynamic_index_in_dim(
            embedded,
            jnp.clip(current_clock_tick - current_section_index, 0, half_microbatch_count - 1),
            0,
            keepdims=False,
        )
        up_row = lax.dynamic_index_in_dim(
            embedded,
            half_microbatch_count
            + jnp.clip(
                current_clock_tick - (final_section - current_section_index),
                0,
                half_microbatch_count - 1,
            ),
            0,
            keepdims=False,
        )
        emb_pair = jnp.stack([down_row, up_row])
        inv_rms, normed, padded, pre_act, active = prepare(inputs, emb_pair, conv_pair)
        outputs = (
            inputs.astype(jnp.float32)
            + jnp.einsum("dfpc,dcx->dfpx", active, out_pair, preferred_element_type=jnp.float32)
        ).astype(jnp.bfloat16)
        saved.append((inv_rms, normed, padded, pre_act, active))
        if current_clock_tick + 1 < ticks:
            down_buf = from_behind(outputs[0], "pipe", 1)
            up_buf = from_behind(outputs[1], "pipe", -1)
    stored = jax.tree.map(lambda *leaves: jnp.stack(leaves), *saved)
    conv_acc = jnp.zeros((2, 3, channels, channels), jnp.float32)
    out_acc = jnp.zeros((2, channels, channels), jnp.float32)
    downward_gradient_holder = empty_activation
    upward_gradient_holder = empty_activation
    for current_clock_tick in range(ticks):
        down_micro = current_clock_tick - (final_section - current_section_index)
        up_micro = current_clock_tick - current_section_index
        down_valid = (down_micro >= 0) & (down_micro < half_microbatch_count)
        up_valid = (up_micro >= 0) & (up_micro < half_microbatch_count)
        downward_hidden_gradient = downward_gradient_holder
        upward_hidden_gradient = upward_gradient_holder
        if current_clock_tick < half_microbatch_count:
            downward_hidden_gradient = jnp.where(
                current_section_index == final_section,
                cotangent[current_clock_tick, 0],
                downward_gradient_holder,
            )
            upward_hidden_gradient = jnp.where(
                current_section_index == 0,
                cotangent[half_microbatch_count + current_clock_tick, 0],
                upward_gradient_holder,
            )
        downward_hidden_gradient = jnp.where(down_valid, downward_hidden_gradient, empty_activation)
        upward_hidden_gradient = jnp.where(up_valid, upward_hidden_gradient, empty_activation)
        grad_out = jnp.stack([downward_hidden_gradient, upward_hidden_gradient])
        down_tick = down_micro + current_section_index
        up_tick = up_micro + final_section - current_section_index
        inv_rms, normed, padded, pre_act, active = tuple(
            (pick(item, down_tick, up_tick) for item in stored)
        )
        out_acc = out_acc + jnp.einsum(
            "dfpc,dfpx->dcx", active, grad_out, preferred_element_type=jnp.float32
        )
        grad_act = jnp.einsum(
            "dfpx,dcx->dfpc", grad_out, out_pair, preferred_element_type=jnp.float32
        )
        sigma = jax.nn.sigmoid(pre_act)
        grad_pre = (grad_act * sigma * (1.0 + pre_act * (1.0 - sigma))).astype(jnp.bfloat16)
        grad_pad = padded_2(grad_pre, (("tm", 1),), 1)
        conv_terms = []
        grad_norm = jnp.zeros(normed.shape, jnp.float32)
        for offset in range(3):
            conv_terms.append(
                jnp.einsum(
                    "dfpc,dfpx->dcx",
                    padded[:, offset : offset + frames],
                    grad_pre,
                    preferred_element_type=jnp.float32,
                )
            )
            grad_norm = grad_norm + jnp.einsum(
                "dfpx,dcx->dfpc",
                grad_pad[:, 2 - offset : 2 - offset + frames],
                conv_pair[:, offset],
                preferred_element_type=jnp.float32,
            )
        conv_acc = conv_acc + jnp.stack(conv_terms, 1)
        incoming_gradient = grad_out.astype(jnp.float32) + inv_rms * (
            grad_norm - normed * jnp.mean(grad_norm * normed, -1, keepdims=True)
        )
        incoming_gradient = incoming_gradient.astype(jnp.bfloat16)
        if current_clock_tick + 1 < ticks:
            downward_gradient_holder = from_behind(incoming_gradient[0], "pipe", -1)
            upward_gradient_holder = from_behind(incoming_gradient[1], "pipe", 1)
    down_total = jnp.concatenate([conv_acc[0], out_acc[0][None]], 0)
    up_total = jnp.concatenate([conv_acc[1], out_acc[1][None]], 0)
    down_sum, up_sum = lax.psum((down_total, up_total), ("tm", "dp"))
    value = up_sum
    for bit_pos in range(bit_count):
        value = from_partner(value.astype(jnp.bfloat16), "pipe", bit_pos).astype(value.dtype)
    total = down_sum + value
    row_count = (
        micro * video.shape[1] * lax.axis_size("dp") * frames * lax.axis_size("tm") * video.shape[3]
    )
    scale = 1.0 / math.sqrt(row_count)
    return ((total[:3] * scale)[None], (total[3] * scale)[None])


def solution(mesh):
    return jax.shard_map(
        body,
        mesh=mesh,
        in_specs=(
            P(None, "dp", "tm", None, None),
            P(None, "dp", "tm", None, None),
            P(None, "dp"),
            P("pipe", None, None, None),
            P("pipe", None, None),
        ),
        out_specs=(P("pipe", None, None, None), P("pipe", None, None)),
        check_vma=False,
    )
```

profile of v0, /device:TPU:24, one launch (start us, length us, event | category | flops | bytes accessed | tf_op | source)
XLA Modules:
  0.0 1158.5 jit_solution(2011999744393750065)
XLA Ops:
  8.5 10.8 collective-permute-start.1
  22.8 3.5 collective-permute-start.2
  26.7 21.4 %collective-permute-done.2 = bf16[4,320,320]{2,1,0:T(8,128)(2,1)} collective-permute-done((bf16[4,320,320]{2,1,0:T(8,128)(2,1)S(1)}, bf16[4,320,320]{2,1,0:T(8,128)(2,1)}, u32[]{:S(2)}, u32[]{:S(2)}) %collective-permute-start.2) | collective-permute-done | bytes 819232 | tf_op jit(solution)/shard_map/ppermute | solution.py:26
  48.1 4.9 collective-permute-start.3
  53.4 20.6 %collective-permute-done.3 = bf16[4,320,320]{2,1,0:T(8,128)(2,1)S(1)} collective-permute-done((bf16[4,320,320]{2,1,0:T(8,128)(2,1)}, bf16[4,320,320]{2,1,0:T(8,128)(2,1)S(1)}, u32[]{:S(2)}, u32[]{:S(2)}) %collective-permute-start.3) | collective-permute-done | bytes 819232 | tf_op jit(solution)/shard_map/ppermute | solution.py:26
  77.8 3.4 collective-permute-start.4
  83.4 4.3 collective-permute-done.5
  90.4 6.0 collective-permute-start.7
  99.4 3.4 collective-permute-start.8
  105.0 4.3 collective-permute-done.9
  111.9 6.4 collective-permute-start.11
  121.3 3.1 collective-permute-start.12
  126.6 4.3 collective-permute-done.13
  133.5 6.4 collective-permute-start.15
  147.0 4.3 collective-permute-done.17
  151.9 6.4 collective-permute-start.19
  160.6 6.3 collective-permute-done.18
  171.8 6.2 collective-permute-start.20
  181.9 4.6 collective-permute-start.23
  192.7 6.4 collective-permute-start.24
  203.6 4.9 collective-permute-start.27
  214.0 6.4 collective-permute-start.28
  225.3 5.2 collective-permute-start.31
  236.7 6.2 collective-permute-start.32
  247.7 5.0 collective-permute-start.35
  252.8 2.2 collective-permute-done.35
  259.1 641.5 %all-reduce.4 = bf16[4,320,320]{2,1,0:T(8,128)(2,1)} all-reduce(f32[4,320,320]{2,1,0:T(8,128)S(1)} %pad_maximum_fusion.1), channel_id=1, replica_groups=mesh['pipe'=4,'tm'=32,'dp'=4] {'tm','dp'}, use_global_device_ids=true, to_apply=%region_10.11 | all-reduce | flops 409600 | bytes 2457600 | tf_op jit(solution)/shard_map/psum | solution.py:198
  900.6 3.7 collective-permute-start.36
  904.3 2.5 pad_maximum_fusion
  906.8 12.7 %collective-permute-done.36 = bf16[4,320,320]{2,1,0:T(8,128)(2,1)S(1)} collective-permute-done((bf16[4,320,320]{2,1,0:T(8,128)(2,1)}, bf16[4,320,320]{2,1,0:T(8,128)(2,1)S(1)}, u32[]{:S(2)}, u32[]{:S(2)}) %collective-permute-start.36) | collective-permute-done | bytes 819232 | tf_op jit(solution)/shard_map/ppermute | solution.py:26
  919.5 10.0 collective-permute-start.37
  929.5 218.4 %all-reduce.3.cloned.1.call-done = f32[4,320,320]{2,1,0:T(8,128)} async-done(((f32[4,320,320]{2,1,0:T(8,128)}), f32[4,320,320]{2,1,0:T(8,128)}) %all-reduce.3.cloned.1.call-update) | async-done | bytes 1638416 | tf_op jit(solution)/shard_map/psum | solution.py:198
  (217 shorter events, 87.1 us)
Async XLA Ops:
  7.2 1140.7 %all-reduce.3.cloned.1.call-start = ((), (), s32[]{:S(2)}) async-start(), calls=%async_computation | async-start | bytes 3932160 | tf_op jit(solution)/shard_map/psum | solution.py:198
  8.5 44.8 %collective-permute-start.1 = (bf16[2,1,64,320]{3,2,1,0:T(8,128)(2,1)S(1)}, bf16[2,1,64,320]{3,2,1,0:T(8,128)(2,1)S(1)}, u32[]{:S(2)}, u32[]{:S(2)}) collective-permute-start(bf16[2,1,64,320]{3,2,1,0:T(8,128)(2,1)S(1)} %get-tuple-element.91), channel_id=1, source_target_pairs={{4,0},{8,4},{12,8},{16,12},{20,16},{24,20},{28,24},{32,28},{36,32}... | collective-permute-start | bytes 245768 | tf_op jit(solution)/shard_map/ppermute | solution.py:18
  19.4 34.0 %collective-permute-start = (bf16[2,1,64,320]{3,2,1,0:T(8,128)(2,1)S(1)}, bf16[2,1,64,320]{3,2,1,0:T(8,128)(2,1)S(1)}, u32[]{:S(2)}, u32[]{:S(2)}) collective-permute-start(bf16[2,1,64,320]{3,2,1,0:T(8,128)(2,1)S(1)} %get-tuple-element.92), channel_id=1, source_target_pairs={{0,4},{4,8},{8,12},{12,16},{16,20},{20,24},{24,28},{28,32},{32,36}... | collective-permute-start | bytes 245768 | tf_op jit(solution)/shard_map/ppermute | solution.py:15
  22.8 25.3 %collective-permute-start.2 = (bf16[4,320,320]{2,1,0:T(8,128)(2,1)S(1)}, bf16[4,320,320]{2,1,0:T(8,128)(2,1)}, u32[]{:S(2)}, u32[]{:S(2)}) collective-permute-start(bf16[4,320,320]{2,1,0:T(8,128)(2,1)S(1)} %pad_maximum_fusion.2), channel_id=1, source_target_pairs={{0,128},{128,0},{256,384},{384,256},{1,129},{129,1},{257,385},{385... | collective-permute-start | bytes 2457608 | tf_op jit(solution)/shard_map/ppermute | solution.py:26
  48.1 25.9 %collective-permute-start.3 = (bf16[4,320,320]{2,1,0:T(8,128)(2,1)}, bf16[4,320,320]{2,1,0:T(8,128)(2,1)S(1)}, u32[]{:S(2)}, u32[]{:S(2)}) collective-permute-start(bf16[4,320,320]{2,1,0:T(8,128)(2,1)} %collective-permute-done.2), channel_id=1, source_target_pairs={{0,256},{128,384},{256,0},{384,128},{1,257},{129,385},{257,1},{385... | collective-permute-start | bytes 2457608 | tf_op jit(solution)/shard_map/ppermute | solution.py:26
  81.2 6.5 collective-permute-start.5
  88.4 8.6 collective-permute-start.6
  90.4 8.2 collective-permute-start.7
  102.8 6.5 collective-permute-start.9
  109.9 9.0 collective-permute-start.10
  111.9 8.6 collective-permute-start.11
  131.5 9.0 collective-permute-start.14
  133.5 8.6 collective-permute-start.15
  151.9 15.3 %collective-permute-start.19 = (bf16[2,1,64,320]{3,2,1,0:T(8,128)(2,1)S(1)}, bf16[2,1,64,320]{3,2,1,0:T(8,128)(2,1)S(1)}, u32[]{:S(2)}, u32[]{:S(2)}) collective-permute-start(bf16[2,1,64,320]{3,2,1,0:T(8,128)(2,1)S(1)} %get-tuple-element.75), channel_id=1, source_target_pairs={{4,0},{8,4},{12,8},{16,12},{20,16},{24,20},{28,24},{32,28},{36,32}... | collective-permute-start | bytes 245768 | tf_op jit(solution)/shard_map/ppermute | solution.py:18
  158.3 8.6 collective-permute-start.18
  169.6 8.6 collective-permute-start.21
  171.8 8.2 collective-permute-start.20
  181.9 6.8 collective-permute-start.23
  189.8 9.4 collective-permute-start.25
  192.7 8.6 collective-permute-start.24
  201.9 6.9 collective-permute-start.26
  203.6 7.1 collective-permute-start.27
  211.8 9.2 collective-permute-start.29
  214.0 9.1 collective-permute-start.28
  223.7 7.9 collective-permute-start.30
  225.3 8.1 collective-permute-start.31
  234.5 8.8 collective-permute-start.33
  236.7 8.4 collective-permute-start.32
  245.8 7.0 collective-permute-start.34
  247.7 7.2 collective-permute-start.35
  900.6 18.9 %collective-permute-start.36 = (bf16[4,320,320]{2,1,0:T(8,128)(2,1)}, bf16[4,320,320]{2,1,0:T(8,128)(2,1)S(1)}, u32[]{:S(2)}, u32[]{:S(2)}) collective-permute-start(bf16[4,320,320]{2,1,0:T(8,128)(2,1)} %all-reduce.4), channel_id=1, source_target_pairs={{0,128},{128,0},{256,384},{384,256},{1,129},{129,1},{257,385},{385... | collective-permute-start | bytes 2457608 | tf_op jit(solution)/shard_map/ppermute | solution.py:26
  919.5 228.5 %collective-permute-start.37 = (bf16[4,320,320]{2,1,0:T(8,128)(2,1)S(1)}, bf16[4,320,320]{2,1,0:T(8,128)(2,1)S(1)}, u32[]{:S(2)}, u32[]{:S(2)}) collective-permute-start(bf16[4,320,320]{2,1,0:T(8,128)(2,1)S(1)} %collective-permute-done.36), channel_id=1, source_target_pairs={{0,256},{128,384},{256,0},{384,128},{1,257},{129,385},{257,1},{385... | collective-permute-start | bytes 2457608 | tf_op jit(solution)/shard_map/ppermute | solution.py:26
  (13 other events, 169.7 us)
Sparse Core Ops, SparseCore 0:
  906.9 240.9 all-reduce.2
where the time goes:
time: 1160 us
  blocking collectives  641 us (55%)
  waiting for transfers between devices  323 us (28%)
  starting transfers between devices  143 us (12%)
  matrix products  18.2 us (2%)
  between operations  15.5 us (1%)
  other arithmetic  13.4 us (1%)
    psum x1, blocking collectives, body(): down_sum, up_sum = lax.psum((down_total, up_total), ('tm', 'dp'))  641 us
    psum x1, waiting for transfers between devices, body(): down_sum, up_sum = lax.psum((down_total, up_total), ('tm', 'dp'))  218 us
    ppermute x9, starting transfers between devices, padded_2(): lax.ppermute(lax.slice_in_dim(block, 0, width, axis=dim), axis, backward)  61.4 us
    ppermute x4, waiting for transfers between devices, from_partner(): return lax.ppermute(value, axis, pairs)  54.6 us
    ppermute x16, starting transfers between devices, from_behind(): return lax.ppermute(array, axis, pairs)  41.9 us
    ppermute x16, waiting for transfers between devices, from_behind(): return lax.ppermute(array, axis, pairs)  29.7 us
  transfers between devices with their start and end apart: 39, of which 33 were waited for; matrix products, arithmetic and copies ran while one was open for 1% of the time, Pallas kernels for 0%

commit v1 on v0

--- a/solution.py
+++ b/solution.py
@@ -195,7 +195,7 @@
             upward_gradient_holder = from_behind(incoming_gradient[1], "pipe", 1)
     down_total = jnp.concatenate([conv_acc[0], out_acc[0][None]], 0)
     up_total = jnp.concatenate([conv_acc[1], out_acc[1][None]], 0)
-    down_sum, up_sum = lax.psum((down_total, up_total), ("tm", "dp"))
+    down_sum, up_sum = lax.psum(lax.psum((down_total, up_total), "tm"), "dp")
     value = up_sum
     for bit_pos in range(bit_count):
         value = from_partner(value.astype(jnp.bfloat16), "pipe", bit_pos).astype(value.dtype)

time: 1160 us -> 743 us (0.64)
  the two profiles are of different devices: /device:TPU:24 before, /device:TPU:56 now
where the time goes in v1:
time: 743 us; the launch traced here: 742 us
  waiting for transfers between devices  449 us (60%)
  starting transfers between devices  138 us (19%)
  blocking collectives  104 us (14%)
  matrix products  18.3 us (2%)
  between operations  15.5 us (2%)
  other arithmetic  13.1 us (2%)
    psum x2, waiting for transfers between devices, body(): down_sum, up_sum = lax.psum(lax.psum((down_total, up_total), 'tm'), 'dp')  324 us
    psum x1, blocking collectives, body(): down_sum, up_sum = lax.psum(lax.psum((down_total, up_total), 'tm'), 'dp')  104 us
    ppermute x4, waiting for transfers between devices, from_partner(): return lax.ppermute(value, axis, pairs)  75.7 us
    ppermute x9, starting transfers between devices, padded_2(): lax.ppermute(lax.slice_in_dim(block, 0, width, axis=dim), axis, backward)  62.3 us
    ppermute x16, starting transfers between devices, from_behind(): return lax.ppermute(array, axis, pairs)  41.9 us
    ppermute x16, waiting for transfers between devices, from_behind(): return lax.ppermute(array, axis, pairs)  29.8 us
    ppermute x9, starting transfers between devices, padded_2(): lax.ppermute(lax.slice_in_dim(block, block.shape[dim] - width, None, axis...  17.3 us
    ppermute x4, starting transfers between devices, from_partner(): return lax.ppermute(value, axis, pairs)  16.7 us
  transfers between devices with their start and end apart: 40, of which 35 were waited for; matrix products, arithmetic and copies ran while one was open for 1% of the time, Pallas kernels for 0%

profile of v1, /device:TPU:56, one launch (start us, length us, event | category | flops | bytes accessed | tf_op | source)
XLA Modules:
  0.0 742.1 jit_solution(5268657340023033214)
XLA Ops:
  8.5 11.7 %collective-permute-start.1 = (bf16[2,1,64,320]{3,2,1,0:T(8,128)(2,1)S(1)}, bf16[2,1,64,320]{3,2,1,0:T(8,128)(2,1)S(1)}, u32[]{:S(2)}, u32[]{:S(2)}) collective-permute-start(bf16[2,1,64,320]{3,2,1,0:T(8,128)(2,1)S(1)} %get-tuple-element.93), channel_id=1, source_target_pairs={{4,0},{8,4},{12,8},{16,12},{20,16},{24,20},{28,24},{32,28},{36,32}... | collective-permute-start | bytes 245768 | tf_op jit(solution)/shard_map/ppermute | solution.py:18
  23.6 3.5 collective-permute-start.2
  27.6 21.4 %collective-permute-done.2 = bf16[4,320,320]{2,1,0:T(8,128)(2,1)} collective-permute-done((bf16[4,320,320]{2,1,0:T(8,128)(2,1)S(1)}, bf16[4,320,320]{2,1,0:T(8,128)(2,1)}, u32[]{:S(2)}, u32[]{:S(2)}) %collective-permute-start.2) | collective-permute-done | bytes 819232 | tf_op jit(solution)/shard_map/ppermute | solution.py:26
  49.0 4.9 collective-permute-start.3
  54.3 20.6 %collective-permute-done.3 = bf16[4,320,320]{2,1,0:T(8,128)(2,1)S(1)} collective-permute-done((bf16[4,320,320]{2,1,0:T(8,128)(2,1)}, bf16[4,320,320]{2,1,0:T(8,128)(2,1)S(1)}, u32[]{:S(2)}, u32[]{:S(2)}) %collective-permute-start.3) | collective-permute-done | bytes 819232 | tf_op jit(solution)/shard_map/ppermute | solution.py:26
  76.9 3.4 collective-permute-start.4
  82.5 4.3 collective-permute-done.5
  89.5 6.0 collective-permute-start.7
  98.5 3.4 collective-permute-start.8
  104.1 4.3 collective-permute-done.9
  111.0 6.4 collective-permute-start.11
  120.4 3.1 collective-permute-start.12
  125.7 4.3 collective-permute-done.13
  132.6 6.4 collective-permute-start.15
  146.1 4.3 collective-permute-done.17
  151.0 6.4 collective-permute-start.19
  159.7 6.3 collective-permute-done.18
  170.9 6.2 collective-permute-start.20
  181.0 4.6 collective-permute-start.23
  191.8 6.4 collective-permute-start.24
  202.7 4.9 collective-permute-start.27
  213.1 6.4 collective-permute-start.28
  224.4 5.2 collective-permute-start.31
  235.9 6.2 collective-permute-start.32
  246.9 5.0 collective-permute-start.35
  259.8 314.2 %all-reduce.7.cloned.1.call-done = (f32[4,320,320]{2,1,0:T(8,128)}, f32[4,320,320]{2,1,0:T(8,128)}) async-done(((f32[4,320,320]{2,1,0:T(8,128)}, f32[4,320,320]{2,1,0:T(8,128)}), (f32[4,320,320]{2,1,0:T(8,128)}, f32[4,320,320]{2,1,0:T(8,128)})) %all-reduce.7.cloned.1.call-update) | async-done | bytes 3276816 | tf_op jit(solution)/shard_map/psum | solution.py:198
  575.5 104.1 %all-reduce.8 = bf16[4,320,320]{2,1,0:T(8,128)(2,1)S(1)} all-reduce(f32[4,320,320]{2,1,0:T(8,128)S(1)} %copy-done.1), channel_id=1, replica_groups=mesh['pipe'=4,'tm'=32,'dp'=4] {'dp'}, use_global_device_ids=true, to_apply=%region_12.13 | all-reduce | flops 409600 | bytes 2457600 | tf_op jit(solution)/shard_map/psum | solution.py:198
  679.6 3.4 collective-permute-start.36
  683.0 22.2 %collective-permute-done.36 = bf16[4,320,320]{2,1,0:T(8,128)(2,1)S(1)} collective-permute-done((bf16[4,320,320]{2,1,0:T(8,128)(2,1)S(1)}, bf16[4,320,320]{2,1,0:T(8,128)(2,1)S(1)}, u32[]{:S(2)}, u32[]{:S(2)}) %collective-permute-start.36) | collective-permute-done | bytes 819232 | tf_op jit(solution)/shard_map/ppermute | solution.py:26
  705.2 4.9 collective-permute-start.37
  710.1 9.9 %all-reduce.5.cloned.1.call-done = f32[4,320,320]{2,1,0:T(8,128)} async-done(((f32[4,320,320]{2,1,0:T(8,128)}), f32[4,320,320]{2,1,0:T(8,128)}) %all-reduce.5.cloned.1.call-update) | async-done | bytes 1638416 | tf_op jit(solution)/shard_map/psum | solution.py:198
  720.0 11.5 %collective-permute-done.37 = bf16[4,320,320]{2,1,0:T(8,128)(2,1)S(1)} collective-permute-done((bf16[4,320,320]{2,1,0:T(8,128)(2,1)S(1)}, bf16[4,320,320]{2,1,0:T(8,128)(2,1)S(1)}, u32[]{:S(2)}, u32[]{:S(2)}) %collective-permute-start.37) | collective-permute-done | bytes 819232 | tf_op jit(solution)/shard_map/ppermute | solution.py:26
  (219 shorter events, 90.5 us)
Async XLA Ops:
  7.2 566.8 %all-reduce.7.cloned.1.call-start = ((), (), s32[]{:S(2)}) async-start(), calls=%async_computation.1 | async-start | bytes 7864320 | tf_op jit(solution)/shard_map/psum | solution.py:198
  8.5 45.7 %collective-permute-start.1 = (bf16[2,1,64,320]{3,2,1,0:T(8,128)(2,1)S(1)}, bf16[2,1,64,320]{3,2,1,0:T(8,128)(2,1)S(1)}, u32[]{:S(2)}, u32[]{:S(2)}) collective-permute-start(bf16[2,1,64,320]{3,2,1,0:T(8,128)(2,1)S(1)} %get-tuple-element.93), channel_id=1, source_target_pairs={{4,0},{8,4},{12,8},{16,12},{20,16},{24,20},{28,24},{32,28},{36,32}... | collective-permute-start | bytes 245768 | tf_op jit(solution)/shard_map/ppermute | solution.py:18
  20.3 34.0 %collective-permute-start = (bf16[2,1,64,320]{3,2,1,0:T(8,128)(2,1)S(1)}, bf16[2,1,64,320]{3,2,1,0:T(8,128)(2,1)S(1)}, u32[]{:S(2)}, u32[]{:S(2)}) collective-permute-start(bf16[2,1,64,320]{3,2,1,0:T(8,128)(2,1)S(1)} %get-tuple-element.94), channel_id=1, source_target_pairs={{0,4},{4,8},{8,12},{12,16},{16,20},{20,24},{24,28},{28,32},{32,36}... | collective-permute-start | bytes 245768 | tf_op jit(solution)/shard_map/ppermute | solution.py:15
  23.6 25.3 %collective-permute-start.2 = (bf16[4,320,320]{2,1,0:T(8,128)(2,1)S(1)}, bf16[4,320,320]{2,1,0:T(8,128)(2,1)}, u32[]{:S(2)}, u32[]{:S(2)}) collective-permute-start(bf16[4,320,320]{2,1,0:T(8,128)(2,1)S(1)} %pad_maximum_fusion.2), channel_id=1, source_target_pairs={{0,128},{128,0},{256,384},{384,256},{1,129},{129,1},{257,385},{385... | collective-permute-start | bytes 2457608 | tf_op jit(solution)/shard_map/ppermute | solution.py:26
  49.0 25.9 %collective-permute-start.3 = (bf16[4,320,320]{2,1,0:T(8,128)(2,1)}, bf16[4,320,320]{2,1,0:T(8,128)(2,1)S(1)}, u32[]{:S(2)}, u32[]{:S(2)}) collective-permute-start(bf16[4,320,320]{2,1,0:T(8,128)(2,1)} %collective-permute-done.2), channel_id=1, source_target_pairs={{0,256},{128,384},{256,0},{384,128},{1,257},{129,385},{257,1},{385... | collective-permute-start | bytes 2457608 | tf_op jit(solution)/shard_map/ppermute | solution.py:26
  87.5 8.6 %collective-permute-start.6 = (bf16[2,1,64,320]{3,2,1,0:T(8,128)(2,1)S(1)}, bf16[2,1,64,320]{3,2,1,0:T(8,128)(2,1)S(1)}, u32[]{:S(2)}, u32[]{:S(2)}) collective-permute-start(bf16[2,1,64,320]{3,2,1,0:T(8,128)(2,1)S(1)} %get-tuple-element.90), channel_id=1, source_target_pairs={{0,4},{4,8},{8,12},{12,16},{16,20},{20,24},{24,28},{28,32},{32,36}... | collective-permute-start | bytes 245768 | tf_op jit(solution)/shard_map/ppermute | solution.py:15
  89.5 8.2 %collective-permute-start.7 = (bf16[2,1,64,320]{3,2,1,0:T(8,128)(2,1)S(1)}, bf16[2,1,64,320]{3,2,1,0:T(8,128)(2,1)S(1)}, u32[]{:S(2)}, u32[]{:S(2)}) collective-permute-start(bf16[2,1,64,320]{3,2,1,0:T(8,128)(2,1)S(1)} %get-tuple-element.89), channel_id=1, source_target_pairs={{4,0},{8,4},{12,8},{16,12},{20,16},{24,20},{28,24},{32,28},{36,32}... | collective-permute-start | bytes 245768 | tf_op jit(solution)/shard_map/ppermute | solution.py:18
  101.9 6.5 collective-permute-start.9
  109.0 9.0 %collective-permute-start.10 = (bf16[2,1,64,320]{3,2,1,0:T(8,128)(2,1)S(1)}, bf16[2,1,64,320]{3,2,1,0:T(8,128)(2,1)S(1)}, u32[]{:S(2)}, u32[]{:S(2)}) collective-permute-start(bf16[2,1,64,320]{3,2,1,0:T(8,128)(2,1)S(1)} %get-tuple-element.86), channel_id=1, source_target_pairs={{0,4},{4,8},{8,12},{12,16},{16,20},{20,24},{24,28},{28,32},{32,36}... | collective-permute-start | bytes 245768 | tf_op jit(solution)/shard_map/ppermute | solution.py:15
  111.0 8.6 %collective-permute-start.11 = (bf16[2,1,64,320]{3,2,1,0:T(8,128)(2,1)S(1)}, bf16[2,1,64,320]{3,2,1,0:T(8,128)(2,1)S(1)}, u32[]{:S(2)}, u32[]{:S(2)}) collective-permute-start(bf16[2,1,64,320]{3,2,1,0:T(8,128)(2,1)S(1)} %get-tuple-element.85), channel_id=1, source_target_pairs={{4,0},{8,4},{12,8},{16,12},{20,16},{24,20},{28,24},{32,28},{36,32}... | collective-permute-start | bytes 245768 | tf_op jit(solution)/shard_map/ppermute | solution.py:18
  130.6 9.0 %collective-permute-start.14 = (bf16[2,1,64,320]{3,2,1,0:T(8,128)(2,1)S(1)}, bf16[2,1,64,320]{3,2,1,0:T(8,128)(2,1)S(1)}, u32[]{:S(2)}, u32[]{:S(2)}) collective-permute-start(bf16[2,1,64,320]{3,2,1,0:T(8,128)(2,1)S(1)} %get-tuple-element.82), channel_id=1, source_target_pairs={{0,4},{4,8},{8,12},{12,16},{16,20},{20,24},{24,28},{28,32},{32,36}... | collective-permute-start | bytes 245768 | tf_op jit(solution)/shard_map/ppermute | solution.py:15
  132.6 8.6 %collective-permute-start.15 = (bf16[2,1,64,320]{3,2,1,0:T(8,128)(2,1)S(1)}, bf16[2,1,64,320]{3,2,1,0:T(8,128)(2,1)S(1)}, u32[]{:S(2)}, u32[]{:S(2)}) collective-permute-start(bf16[2,1,64,320]{3,2,1,0:T(8,128)(2,1)S(1)} %get-tuple-element.81), channel_id=1, source_target_pairs={{4,0},{8,4},{12,8},{16,12},{20,16},{24,20},{28,24},{32,28},{36,32}... | collective-permute-start | bytes 245768 | tf_op jit(solution)/shard_map/ppermute | solution.py:18
  151.0 15.3 %collective-permute-start.19 = (bf16[2,1,64,320]{3,2,1,0:T(8,128)(2,1)S(1)}, bf16[2,1,64,320]{3,2,1,0:T(8,128)(2,1)S(1)}, u32[]{:S(2)}, u32[]{:S(2)}) collective-permute-start(bf16[2,1,64,320]{3,2,1,0:T(8,128)(2,1)S(1)} %get-tuple-element.77), channel_id=1, source_target_pairs={{4,0},{8,4},{12,8},{16,12},{20,16},{24,20},{28,24},{32,28},{36,32}... | collective-permute-start | bytes 245768 | tf_op jit(solution)/shard_map/ppermute | solution.py:18
  157.4 8.6 %collective-permute-start.18 = (bf16[2,1,64,320]{3,2,1,0:T(8,128)(2,1)S(1)}, bf16[2,1,64,320]{3,2,1,0:T(8,128)(2,1)S(1)}, u32[]{:S(2)}, u32[]{:S(2)}) collective-permute-start(bf16[2,1,64,320]{3,2,1,0:T(8,128)(2,1)S(1)} %get-tuple-element.78), channel_id=1, source_target_pairs={{0,4},{4,8},{8,12},{12,16},{16,20},{20,24},{24,28},{28,32},{32,36}... | collective-permute-start | bytes 245768 | tf_op jit(solution)/shard_map/ppermute | solution.py:15
  168.6 8.6 %collective-permute-start.21 = (bf16[2,1,64,320]{3,2,1,0:T(8,128)(2,1)S(1)}, bf16[2,1,64,320]{3,2,1,0:T(8,128)(2,1)S(1)}, u32[]{:S(2)}, u32[]{:S(2)}) collective-permute-start(bf16[2,1,64,320]{3,2,1,0:T(8,128)(2,1)S(1)} %get-tuple-element.76), channel_id=1, source_target_pairs={{0,4},{4,8},{8,12},{12,16},{16,20},{20,24},{24,28},{28,32},{32,36}... | collective-permute-start | bytes 245768 | tf_op jit(solution)/shard_map/ppermute | solution.py:15
  170.9 8.2 %collective-permute-start.20 = (bf16[2,1,64,320]{3,2,1,0:T(8,128)(2,1)S(1)}, bf16[2,1,64,320]{3,2,1,0:T(8,128)(2,1)S(1)}, u32[]{:S(2)}, u32[]{:S(2)}) collective-permute-start(bf16[2,1,64,320]{3,2,1,0:T(8,128)(2,1)S(1)} %get-tuple-element.75), channel_id=1, source_target_pairs={{4,0},{8,4},{12,8},{16,12},{20,16},{24,20},{28,24},{32,28},{36,32}... | collective-permute-start | bytes 245768 | tf_op jit(solution)/shard_map/ppermute | solution.py:18
  181.0 6.8 collective-permute-start.23
  188.8 9.4 %collective-permute-start.25 = (bf16[2,1,64,320]{3,2,1,0:T(8,128)(2,1)S(1)}, bf16[2,1,64,320]{3,2,1,0:T(8,128)(2,1)S(1)}, u32[]{:S(2)}, u32[]{:S(2)}) collective-permute-start(bf16[2,1,64,320]{3,2,1,0:T(8,128)(2,1)S(1)} %get-tuple-element.72), channel_id=1, source_target_pairs={{0,4},{4,8},{8,12},{12,16},{16,20},{20,24},{24,28},{28,32},{32,36}... | collective-permute-start | bytes 245768 | tf_op jit(solution)/shard_map/ppermute | solution.py:15
  191.8 8.6 %collective-permute-start.24 = (bf16[2,1,64,320]{3,2,1,0:T(8,128)(2,1)S(1)}, bf16[2,1,64,320]{3,2,1,0:T(8,128)(2,1)S(1)}, u32[]{:S(2)}, u32[]{:S(2)}) collective-permute-start(bf16[2,1,64,320]{3,2,1,0:T(8,128)(2,1)S(1)} %get-tuple-element.71), channel_id=1, source_target_pairs={{4,0},{8,4},{12,8},{16,12},{20,16},{24,20},{28,24},{32,28},{36,32}... | collective-permute-start | bytes 245768 | tf_op jit(solution)/shard_map/ppermute | solution.py:18
  201.0 6.9 collective-permute-start.26
  202.7 7.1 collective-permute-start.27
  210.9 9.2 %collective-permute-start.29 = (bf16[2,1,64,320]{3,2,1,0:T(8,128)(2,1)S(1)}, bf16[2,1,64,320]{3,2,1,0:T(8,128)(2,1)S(1)}, u32[]{:S(2)}, u32[]{:S(2)}) collective-permute-start(bf16[2,1,64,320]{3,2,1,0:T(8,128)(2,1)S(1)} %get-tuple-element.68), channel_id=1, source_target_pairs={{0,4},{4,8},{8,12},{12,16},{16,20},{20,24},{24,28},{28,32},{32,36}... | collective-permute-start | bytes 245768 | tf_op jit(solution)/shard_map/ppermute | solution.py:15
  213.1 9.0 %collective-permute-start.28 = (bf16[2,1,64,320]{3,2,1,0:T(8,128)(2,1)S(1)}, bf16[2,1,64,320]{3,2,1,0:T(8,128)(2,1)S(1)}, u32[]{:S(2)}, u32[]{:S(2)}) collective-permute-start(bf16[2,1,64,320]{3,2,1,0:T(8,128)(2,1)S(1)} %get-tuple-element.67), channel_id=1, source_target_pairs={{4,0},{8,4},{12,8},{16,12},{20,16},{24,20},{28,24},{32,28},{36,32}... | collective-permute-start | bytes 245768 | tf_op jit(solution)/shard_map/ppermute | solution.py:18
  222.7 8.0 %collective-permute-start.30 = (bf16[2,64,320]{2,1,0:T(8,128)(2,1)S(1)}, bf16[2,64,320]{2,1,0:T(8,128)(2,1)S(1)}, u32[]{:S(2)}, u32[]{:S(2)}) collective-permute-start(bf16[2,64,320]{2,1,0:T(8,128)(2,1)S(1)} %get-tuple-element.65), channel_id=1, source_target_pairs={{128,0},{256,128},{384,256},{129,1},{257,129},{385,257},{130,2},{2... | collective-permute-start | bytes 245768 | tf_op jit(solution)/shard_map/ppermute | solution.py:32
  224.4 8.2 %collective-permute-start.31 = (bf16[2,64,320]{2,1,0:T(8,128)(2,1)S(1)}, bf16[2,64,320]{2,1,0:T(8,128)(2,1)S(1)}, u32[]{:S(2)}, u32[]{:S(2)}) collective-permute-start(bf16[2,64,320]{2,1,0:T(8,128)(2,1)S(1)} %get-tuple-element.66), channel_id=1, source_target_pairs={{0,128},{128,256},{256,384},{1,129},{129,257},{257,385},{2,130},{1... | collective-permute-start | bytes 245768 | tf_op jit(solution)/shard_map/ppermute | solution.py:32
  233.6 8.8 %collective-permute-start.33 = (bf16[2,1,64,320]{3,2,1,0:T(8,128)(2,1)S(1)}, bf16[2,1,64,320]{3,2,1,0:T(8,128)(2,1)S(1)}, u32[]{:S(2)}, u32[]{:S(2)}) collective-permute-start(bf16[2,1,64,320]{3,2,1,0:T(8,128)(2,1)S(1)} %get-tuple-element.64), channel_id=1, source_target_pairs={{0,4},{4,8},{8,12},{12,16},{16,20},{20,24},{24,28},{28,32},{32,36}... | collective-permute-start | bytes 245768 | tf_op jit(solution)/shard_map/ppermute | solution.py:15
  235.9 8.4 %collective-permute-start.32 = (bf16[2,1,64,320]{3,2,1,0:T(8,128)(2,1)S(1)}, bf16[2,1,64,320]{3,2,1,0:T(8,128)(2,1)S(1)}, u32[]{:S(2)}, u32[]{:S(2)}) collective-permute-start(bf16[2,1,64,320]{3,2,1,0:T(8,128)(2,1)S(1)} %get-tuple-element.63), channel_id=1, source_target_pairs={{4,0},{8,4},{12,8},{16,12},{20,16},{24,20},{28,24},{32,28},{36,32}... | collective-permute-start | bytes 245768 | tf_op jit(solution)/shard_map/ppermute | solution.py:18
  244.9 7.0 collective-permute-start.34
  246.9 7.2 collective-permute-start.35
  259.7 460.3 %all-reduce.5.cloned.1.call-start = ((), (), s32[]{:S(2)}) async-start(), calls=%async_computation | async-start | bytes 3932160 | tf_op jit(solution)/shard_map/psum | solution.py:198
  679.6 25.6 %collective-permute-start.36 = (bf16[4,320,320]{2,1,0:T(8,128)(2,1)S(1)}, bf16[4,320,320]{2,1,0:T(8,128)(2,1)S(1)}, u32[]{:S(2)}, u32[]{:S(2)}) collective-permute-start(bf16[4,320,320]{2,1,0:T(8,128)(2,1)S(1)} %all-reduce.8), channel_id=1, source_target_pairs={{0,128},{128,0},{256,384},{384,256},{1,129},{129,1},{257,385},{385... | collective-permute-start | bytes 2457608 | tf_op jit(solution)/shard_map/ppermute | solution.py:26
  705.2 26.4 %collective-permute-start.37 = (bf16[4,320,320]{2,1,0:T(8,128)(2,1)S(1)}, bf16[4,320,320]{2,1,0:T(8,128)(2,1)S(1)}, u32[]{:S(2)}, u32[]{:S(2)}) collective-permute-start(bf16[4,320,320]{2,1,0:T(8,128)(2,1)S(1)} %collective-permute-done.36), channel_id=1, source_target_pairs={{0,256},{128,384},{256,0},{384,128},{1,257},{129,385},{257,1},{385... | collective-permute-start | bytes 2457608 | tf_op jit(solution)/shard_map/ppermute | solution.py:26
  (14 other events, 177.8 us)
Sparse Core Ops, SparseCore 0:
  259.8 314.0 all-reduce.6
  577.2 142.7 all-reduce.4
